TPU v7x, 32 devices: a whole 2x2x4 slice. The times are simulated.
32 devices in a mesh: dp: 8 (over z, x), section: 4 (over y, core).
Axes of the slice: x: 2, y: 2, z: 4, core: 2. Of those that a mesh axis runs over, the one named last changes fastest.
Arguments:
- images_in: bfloat16 [2048, 4096], P(('dp', 'section')), may hold values from -6 to 6
- labels: int32 [2048], P(('dp', 'section')), may hold values from 0 to 9
- conv_weight: float32 [3, 2, 576, 64], P(None, None, None, 'section'), may hold values from -0.25 to 0.25
- frn_gain: float32 [3, 2, 64], replicated, may hold values from 0.25 to 1.75
- frn_bias: float32 [3, 2, 64], replicated, may hold values from -3 to 3
- head_weight: float32 [64, 10], replicated, as said below
- head_bias: float32 [10], replicated, may hold values from -4 to 4
Outputs:
- grad_conv: float32 [3, 2, 576, 64], P(None, None, None, 'section')
- grad_norm: float32 [3, 2, 2, 64], replicated
- grad_head_weight: float32 [64, 10], replicated
- grad_head_bias: float32 [10], replicated
Inputs may be any that keep to these rules, and one draw needn't show every extreme that they name: `head_weight`: the classifier's weights.
All inputs are finite; a program needn't handle non-finite values.
Results may differ from a plain program's by a relative error of at most 0.0033.
The roundings to bfloat16 on the way count: a program that leaves them out, or rounds other values in their place, can miss the bound.
Values may be sent and summed in bfloat16 or wider, within the bound.
A program may use at most 64 MiB of HBM per device.

v0:
```python
import jax
import jax.numpy as jnp
from jax import lax
from jax.sharding import PartitionSpec as P

SIDE = 8
MICRO = 8


eps = 1e-06
prior_precision = 0.5


def make_patches(maps):
    side = maps.shape[1]
    padded = jnp.pad(maps, ((0, 0), (1, 1), (1, 1), (0, 0)))
    taps = [padded[:, a : a + side, e : e + side, :] for a in range(3) for e in range(3)]
    stacked = jnp.concatenate(taps, axis=3)
    return stacked.reshape(maps.shape[0] * side * side, 9 * maps.shape[3])


def fold_patches(columns, shape):
    back = jax.vjp(make_patches, jnp.zeros(shape, jnp.float32))[1]
    return back(columns)[0]


def respond(values, gain, bias, count):
    grouped = values.reshape(count, -1, values.shape[1])
    energy = jnp.mean(grouped * grouped, axis=1, keepdims=True)
    normed = grouped * lax.rsqrt(energy + eps)
    return (gain * normed + bias).reshape(values.shape)


def swish(values):
    return values * jax.nn.sigmoid(values)


def block_forward(maps, weights, gains, biases):
    count = maps.shape[0]
    w_first = weights[0]
    w_second = weights[1]
    cols_first = make_patches(maps)
    pre_first = jnp.dot(cols_first, w_first, preferred_element_type=jnp.float32)
    hidden = swish(respond(pre_first, gains[0], biases[0], count)).astype(jnp.bfloat16)
    cols_second = make_patches(hidden.reshape(maps.shape))
    pre_second = jnp.dot(cols_second, w_second, preferred_element_type=jnp.float32)
    skip = maps.reshape(pre_second.shape).astype(jnp.float32)
    result = swish(skip + respond(pre_second, gains[1], biases[1], count)).astype(jnp.bfloat16)
    return (result.reshape(maps.shape), (cols_first, pre_first, cols_second, pre_second))


def block_backward(maps, cotangent, weights, gains, biases):
    count = maps.shape[0]
    w_first = weights[0]
    w_second = weights[1]
    saved = block_forward(maps, weights, gains, biases)[1]
    cols_first, pre_first, cols_second, pre_second = saved

    def second_part(values, skip, gain, bias):
        return swish(skip + respond(values, gain, bias, count))

    def first_part(values, gain, bias):
        return swish(respond(values, gain, bias, count))

    skip = maps.reshape(pre_second.shape).astype(jnp.float32)
    back_second = jax.vjp(second_part, pre_second, skip, gains[1], biases[1])[1]
    d_second, d_skip, dg_second, db_second = back_second(
        cotangent.reshape(pre_second.shape).astype(jnp.float32)
    )
    q_second = d_second.astype(jnp.bfloat16)
    dw_second = jnp.dot(cols_second.T, q_second, preferred_element_type=jnp.float32)
    d_hidden = fold_patches(
        jnp.dot(q_second, w_second.T, preferred_element_type=jnp.float32), maps.shape
    )
    back_first = jax.vjp(first_part, pre_first, gains[0], biases[0])[1]
    d_first, dg_first, db_first = back_first(d_hidden.reshape(pre_first.shape))
    q_first = d_first.astype(jnp.bfloat16)
    dw_first = jnp.dot(cols_first.T, q_first, preferred_element_type=jnp.float32)
    d_input = fold_patches(
        jnp.dot(q_first, w_first.T, preferred_element_type=jnp.float32), maps.shape
    )
    d_maps = (d_skip.reshape(maps.shape) + d_input).astype(jnp.bfloat16)
    d_norm = jnp.stack([jnp.stack([dg_first, db_first]), jnp.stack([dg_second, db_second])])
    return (d_maps, jnp.stack([dw_first, dw_second]), d_norm)


def head_grads(final, labels, head_w, head_b, total):
    count = final.shape[0]
    width = final.shape[3]
    pixels = final.shape[1] * final.shape[2]
    pooled = jnp.mean(final.reshape(count, pixels, width).astype(jnp.float32), axis=1)
    logits = jnp.dot(pooled, head_w, precision=lax.Precision.HIGHEST) + head_b
    top = jnp.max(logits, axis=1, keepdims=True)
    expo = jnp.exp(logits - top)
    probs = expo / jnp.sum(expo, axis=1, keepdims=True)
    onehot = (labels[:, None] == jnp.arange(head_w.shape[1])[None, :]).astype(jnp.float32)
    d_logits = (probs - onehot) / total
    d_head_w = jnp.dot(pooled.T, d_logits, precision=lax.Precision.HIGHEST)
    d_head_b = jnp.sum(d_logits, axis=0)
    d_pooled = jnp.dot(d_logits, head_w.T, precision=lax.Precision.HIGHEST) / pixels
    spread = jnp.broadcast_to(d_pooled[:, None, :], (count, pixels, width))
    return (spread.astype(jnp.bfloat16).reshape(final.shape), d_head_w, d_head_b)


def group_grads(maps, labels, weights, gains, biases, head_w, head_b, total):
    saved = []
    for index in range(weights.shape[0]):
        saved.append(maps)
        maps = block_forward(maps, weights[index], gains[index], biases[index])[0]
    cotangent, d_head_w, d_head_b = head_grads(maps, labels, head_w, head_b, total)
    conv_terms = []
    norm_terms = []
    for index in reversed(range(weights.shape[0])):
        cotangent, d_conv, d_norm = block_backward(
            saved[index], cotangent, weights[index], gains[index], biases[index]
        )
        conv_terms.insert(0, d_conv)
        norm_terms.insert(0, d_norm)
    return (jnp.stack(conv_terms), jnp.stack(norm_terms), d_head_w, d_head_b)


def accumulate(maps, labels, weights, gains, biases, head_w, head_b, total):
    width = weights.shape[3]
    initial = (
        jnp.zeros(weights.shape, jnp.float32),
        jnp.zeros((weights.shape[0], 2, 2, width), jnp.float32),
        jnp.zeros(head_w.shape, jnp.float32),
        jnp.zeros(head_b.shape, jnp.float32),
    )

    def advance(carry, item):
        terms = group_grads(item[0], item[1], weights, gains, biases, head_w, head_b, total)
        return (tuple((left + right for left, right in zip(carry, terms))), None)

    return lax.scan(advance, initial, (maps, labels))[0]


def per_device(images_in, labels, conv_weight, frn_gain, frn_bias, head_weight, head_bias):
    images = images_in.shape[0]
    width = frn_gain.shape[2]
    share = conv_weight.shape[3]
    total = images * lax.axis_size("dp") * lax.axis_size("section")
    offset = lax.axis_index("section") * share
    rounded_share = conv_weight.astype(jnp.bfloat16)
    all_conv = lax.all_gather(rounded_share, "section", axis=3, tiled=True)
    group_size = images // MICRO
    maps = images_in.reshape(MICRO, group_size, SIDE, SIDE, width)
    label_groups = labels.reshape(MICRO, group_size)
    conv_grad, norm_grad, head_w_grad, head_b_grad = accumulate(
        maps, label_groups, all_conv, frn_gain, frn_bias, head_weight, head_bias, total
    )
    summed = lax.psum(conv_grad, ("dp", "section"))
    conv_owned = lax.dynamic_slice_in_dim(summed, offset, share, 3)
    norm_sum, head_w_sum, head_b_sum = lax.psum(
        (norm_grad, head_w_grad, head_b_grad), ("dp", "section")
    )
    params = jnp.stack([frn_gain, frn_bias], axis=2)
    return (
        conv_owned + prior_precision * conv_weight,
        norm_sum + prior_precision * params,
        head_w_sum + prior_precision * head_weight,
        head_b_sum + prior_precision * head_bias,
    )


def solution(mesh):
    return jax.shard_map(
        per_device,
        mesh=mesh,
        in_specs=(
            P(("dp", "section"), None),
            P(("dp", "section")),
            P(None, None, None, "section"),
            P(),
            P(),
            P(),
            P(),
        ),
        out_specs=(P(None, None, None, "section"), P(), P(), P()),
        check_vma=False,
    )
```

profile of v0, /device:TPU:0, one launch (start us, length us, event | category | flops | bytes accessed | tf_op | source)
XLA Modules:
  0.0 816.5 jit_solution(12413973247500979296)
XLA Ops:
  9.6 8.5 %all_gather.3 = bf16[3,2,576,64]{2,3,1,0:T(8,128)(2,1)S(1)} all-gather(bf16[3,2,576,16]{2,3,1,0:T(8,128)(2,1)S(1)} %convert_element_type.386), channel_id=1, replica_groups=mesh['dp'=8,'section'=4] {'section'}, dimensions={3}, use_global_device_ids=true | all-gather | bytes 552960 | tf_op jit(solution)/shard_map/all_gather | solution.py:145
  19.2 659.0 %while.19 = (s32[]{:T(128)}, f32[3,2,576,64]{2,3,1,0:T(8,128)}, f32[3,2,2,64]{3,2,1,0:T(2,128)}, f32[64,10]{0,1:T(8,128)}, f32[10]{0:T(128)}, /*index=5*/bf16[8,...) while((s32[]{:T(128)}, f32[3,2,576,64]{2,3,1,0:T(8,128)}, ...), condition=%wide.region_29.30_spmd.clone, body=%wide.region_0.29_spmd.clone.sunk | while | flops 655682368 | bytes 99941760 | solution.py:135
  27.5 3.8 pad_slice_fusion.54
  37.1 4.0 pad_slice_fusion.55
  56.0 4.0 pad_slice_fusion.57
  69.6 4.0 fusion.302
  73.6 2.2 concatenate.404
  75.8 2.2 concatenate.405
  109.9 3.8 pad_slice_fusion.54
  119.4 4.0 pad_slice_fusion.55
  138.3 4.0 pad_slice_fusion.57
  152.0 4.0 fusion.302
  156.0 2.2 concatenate.404
  192.2 3.8 pad_slice_fusion.54
  201.8 4.0 pad_slice_fusion.55
  220.7 4.0 pad_slice_fusion.57
  234.3 4.0 fusion.302
  238.3 2.2 concatenate.404
  274.6 3.8 pad_slice_fusion.54
  284.2 4.0 pad_slice_fusion.55
  303.1 4.0 pad_slice_fusion.57
  316.7 4.0 fusion.302
  320.7 2.2 concatenate.404
  322.9 2.2 concatenate.405
  356.9 3.8 pad_slice_fusion.54
  366.5 4.0 pad_slice_fusion.55
  385.4 4.0 pad_slice_fusion.57
  399.1 4.0 fusion.302
  403.1 2.2 concatenate.404
  405.3 2.2 concatenate.405
  439.3 3.8 pad_slice_fusion.54
  448.9 4.0 pad_slice_fusion.55
  467.8 4.0 pad_slice_fusion.57
  481.4 4.0 fusion.302
  485.4 2.2 concatenate.404
  487.6 2.2 concatenate.405
  521.7 3.8 pad_slice_fusion.54
  531.3 4.0 pad_slice_fusion.55
  550.2 4.0 pad_slice_fusion.57
  563.8 4.0 fusion.302
  567.8 2.2 concatenate.404
  604.0 3.8 pad_slice_fusion.54
  613.6 4.0 pad_slice_fusion.55
  632.5 4.0 pad_slice_fusion.57
  646.1 4.0 fusion.302
  650.2 2.2 concatenate.404
  678.2 40.8 %all-reduce.51 = (f32[3,2,2,64]{3,2,1,0:T(2,128)S(1)}, f32[64,10]{0,1:T(8,128)S(1)}, f32[10]{0:T(128)S(1)}) all-reduce(f32[3,2,2,64]{3,2,1,0:T(2,128)} %get-tuple-element.157, f32[64,10]{0,1:T(8,128)} %get-tuple-element.158, f32[10]{0:T(128)} %get-tuple-element.159), channel_id=1, replica_groups=mesh['dp'=8,'section'=4] {'dp','section'}, use_global_device_ids=true, to_apply=%region_31.32 | all-reduce | flops 1418 | bytes 11344 | tf_op jit(solution)/shard_map/psum | solution.py:154
  722.8 85.1 %all-reduce.54.cloned.1.call-done = f32[3,2,576,64]{2,3,1,0:T(8,128)} async-done(((f32[3,2,576,64]{2,3,1,0:T(8,128)}), f32[3,2,576,64]{2,3,1,0:T(8,128)}) %all-reduce.54.cloned.1.call-update) | async-done | bytes 884752 | tf_op jit(solution)/shard_map/psum | solution.py:152
  (1643 shorter events, 508.5 us)
Async XLA Ops:
  7.2 10.9 %copy-start.31 = (bf16[64,4096]{1,0:T(8,128)(2,1)S(1)}, bf16[64,4096]{1,0:T(8,128)(2,1)}, u32[]{:S(2)}) copy-start(bf16[64,4096]{1,0:T(8,128)(2,1)} %param.9) | copy-start | bytes 1572868
  7.2 800.7 %all-reduce.54.cloned.1.call-start = ((), (), s32[]{:S(2)}) async-start(), calls=%async_computation | async-start | bytes 1966080 | tf_op jit(solution)/shard_map/psum | solution.py:152
  19.2 4.6 copy-start.7
  19.2 23.2 %copy-start.5 = (bf16[3,2,576,64]{2,3,1,0:T(8,128)(2,1)}, bf16[3,2,576,64]{2,3,1,0:T(8,128)(2,1)S(1)}, u32[]{:S(2)}) copy-start(bf16[3,2,576,64]{2,3,1,0:T(8,128)(2,1)S(1)} %get-tuple-element.949) | copy-start | bytes 1327108 | tf_op jit(solution)/shard_map/while
  21.9 11.3 %copy-start.43 = (f32[64]{0:T(128)}, f32[64]{0:T(128)S(1)}, u32[]{:S(2)}) copy-start(f32[64]{0:T(128)S(1)} %get-tuple-element.737) | copy-start | bytes 772 | tf_op jit(solution)/shard_map/while
  21.9 20.9 %copy-start.40 = (f32[64]{0:T(128)}, f32[64]{0:T(128)S(1)}, u32[]{:S(2)}) copy-start(f32[64]{0:T(128)S(1)} %get-tuple-element.752) | copy-start | bytes 772 | tf_op jit(solution)/shard_map/while
  21.9 5.1 copy-start.11
  101.6 4.6 copy-start.7
  101.6 23.1 %copy-start.5 = (bf16[3,2,576,64]{2,3,1,0:T(8,128)(2,1)}, bf16[3,2,576,64]{2,3,1,0:T(8,128)(2,1)S(1)}, u32[]{:S(2)}) copy-start(bf16[3,2,576,64]{2,3,1,0:T(8,128)(2,1)S(1)} %get-tuple-element.949) | copy-start | bytes 1327108 | tf_op jit(solution)/shard_map/while
  104.2 11.3 %copy-start.43 = (f32[64]{0:T(128)}, f32[64]{0:T(128)S(1)}, u32[]{:S(2)}) copy-start(f32[64]{0:T(128)S(1)} %get-tuple-element.737) | copy-start | bytes 772 | tf_op jit(solution)/shard_map/while
  104.2 20.9 %copy-start.40 = (f32[64]{0:T(128)}, f32[64]{0:T(128)S(1)}, u32[]{:S(2)}) copy-start(f32[64]{0:T(128)S(1)} %get-tuple-element.752) | copy-start | bytes 772 | tf_op jit(solution)/shard_map/while
  104.3 5.1 copy-start.11
  128.8 4.3 copy-start.12
  184.0 4.6 copy-start.7
  184.0 23.1 %copy-start.5 = (bf16[3,2,576,64]{2,3,1,0:T(8,128)(2,1)}, bf16[3,2,576,64]{2,3,1,0:T(8,128)(2,1)S(1)}, u32[]{:S(2)}) copy-start(bf16[3,2,576,64]{2,3,1,0:T(8,128)(2,1)S(1)} %get-tuple-element.949) | copy-start | bytes 1327108 | tf_op jit(solution)/shard_map/while
  186.6 11.3 %copy-start.43 = (f32[64]{0:T(128)}, f32[64]{0:T(128)S(1)}, u32[]{:S(2)}) copy-start(f32[64]{0:T(128)S(1)} %get-tuple-element.737) | copy-start | bytes 772 | tf_op jit(solution)/shard_map/while
  186.6 20.9 %copy-start.40 = (f32[64]{0:T(128)}, f32[64]{0:T(128)S(1)}, u32[]{:S(2)}) copy-start(f32[64]{0:T(128)S(1)} %get-tuple-element.752) | copy-start | bytes 772 | tf_op jit(solution)/shard_map/while
  186.6 5.1 copy-start.11
  211.2 4.3 copy-start.12
  266.3 4.6 copy-start.7
  266.3 23.1 %copy-start.5 = (bf16[3,2,576,64]{2,3,1,0:T(8,128)(2,1)}, bf16[3,2,576,64]{2,3,1,0:T(8,128)(2,1)S(1)}, u32[]{:S(2)}) copy-start(bf16[3,2,576,64]{2,3,1,0:T(8,128)(2,1)S(1)} %get-tuple-element.949) | copy-start | bytes 1327108 | tf_op jit(solution)/shard_map/while
  268.9 11.3 %copy-start.43 = (f32[64]{0:T(128)}, f32[64]{0:T(128)S(1)}, u32[]{:S(2)}) copy-start(f32[64]{0:T(128)S(1)} %get-tuple-element.737) | copy-start | bytes 772 | tf_op jit(solution)/shard_map/while
  269.0 20.9 %copy-start.40 = (f32[64]{0:T(128)}, f32[64]{0:T(128)S(1)}, u32[]{:S(2)}) copy-start(f32[64]{0:T(128)S(1)} %get-tuple-element.752) | copy-start | bytes 772 | tf_op jit(solution)/shard_map/while
  269.0 5.1 copy-start.11
  293.5 4.3 copy-start.12
  348.7 4.6 copy-start.7
  348.7 23.1 %copy-start.5 = (bf16[3,2,576,64]{2,3,1,0:T(8,128)(2,1)}, bf16[3,2,576,64]{2,3,1,0:T(8,128)(2,1)S(1)}, u32[]{:S(2)}) copy-start(bf16[3,2,576,64]{2,3,1,0:T(8,128)(2,1)S(1)} %get-tuple-element.949) | copy-start | bytes 1327108 | tf_op jit(solution)/shard_map/while
  351.3 11.3 %copy-start.43 = (f32[64]{0:T(128)}, f32[64]{0:T(128)S(1)}, u32[]{:S(2)}) copy-start(f32[64]{0:T(128)S(1)} %get-tuple-element.737) | copy-start | bytes 772 | tf_op jit(solution)/shard_map/while
  351.3 20.9 %copy-start.40 = (f32[64]{0:T(128)}, f32[64]{0:T(128)S(1)}, u32[]{:S(2)}) copy-start(f32[64]{0:T(128)S(1)} %get-tuple-element.752) | copy-start | bytes 772 | tf_op jit(solution)/shard_map/while
  351.4 5.1 copy-start.11
  375.9 4.3 copy-start.12
  431.1 4.6 copy-start.7
  431.1 23.1 %copy-start.5 = (bf16[3,2,576,64]{2,3,1,0:T(8,128)(2,1)}, bf16[3,2,576,64]{2,3,1,0:T(8,128)(2,1)S(1)}, u32[]{:S(2)}) copy-start(bf16[3,2,576,64]{2,3,1,0:T(8,128)(2,1)S(1)} %get-tuple-element.949) | copy-start | bytes 1327108 | tf_op jit(solution)/shard_map/while
  433.7 11.3 %copy-start.43 = (f32[64]{0:T(128)}, f32[64]{0:T(128)S(1)}, u32[]{:S(2)}) copy-start(f32[64]{0:T(128)S(1)} %get-tuple-element.737) | copy-start | bytes 772 | tf_op jit(solution)/shard_map/while
  433.7 20.9 %copy-start.40 = (f32[64]{0:T(128)}, f32[64]{0:T(128)S(1)}, u32[]{:S(2)}) copy-start(f32[64]{0:T(128)S(1)} %get-tuple-element.752) | copy-start | bytes 772 | tf_op jit(solution)/shard_map/while
  433.7 5.1 copy-start.11
  458.3 4.3 copy-start.12
  513.4 4.6 copy-start.7
  513.4 23.1 %copy-start.5 = (bf16[3,2,576,64]{2,3,1,0:T(8,128)(2,1)}, bf16[3,2,576,64]{2,3,1,0:T(8,128)(2,1)S(1)}, u32[]{:S(2)}) copy-start(bf16[3,2,576,64]{2,3,1,0:T(8,128)(2,1)S(1)} %get-tuple-element.949) | copy-start | bytes 1327108 | tf_op jit(solution)/shard_map/while
  516.0 11.3 %copy-start.43 = (f32[64]{0:T(128)}, f32[64]{0:T(128)S(1)}, u32[]{:S(2)}) copy-start(f32[64]{0:T(128)S(1)} %get-tuple-element.737) | copy-start | bytes 772 | tf_op jit(solution)/shard_map/while
  516.1 20.9 %copy-start.40 = (f32[64]{0:T(128)}, f32[64]{0:T(128)S(1)}, u32[]{:S(2)}) copy-start(f32[64]{0:T(128)S(1)} %get-tuple-element.752) | copy-start | bytes 772 | tf_op jit(solution)/shard_map/while
  516.1 5.1 copy-start.11
  540.6 4.3 copy-start.12
  595.8 4.6 copy-start.7
  595.8 23.1 %copy-start.5 = (bf16[3,2,576,64]{2,3,1,0:T(8,128)(2,1)}, bf16[3,2,576,64]{2,3,1,0:T(8,128)(2,1)S(1)}, u32[]{:S(2)}) copy-start(bf16[3,2,576,64]{2,3,1,0:T(8,128)(2,1)S(1)} %get-tuple-element.949) | copy-start | bytes 1327108 | tf_op jit(solution)/shard_map/while
  598.4 11.3 %copy-start.43 = (f32[64]{0:T(128)}, f32[64]{0:T(128)S(1)}, u32[]{:S(2)}) copy-start(f32[64]{0:T(128)S(1)} %get-tuple-element.737) | copy-start | bytes 772 | tf_op jit(solution)/shard_map/while
  598.4 20.9 %copy-start.40 = (f32[64]{0:T(128)}, f32[64]{0:T(128)S(1)}, u32[]{:S(2)}) copy-start(f32[64]{0:T(128)S(1)} %get-tuple-element.752) | copy-start | bytes 772 | tf_op jit(solution)/shard_map/while
  598.5 5.1 copy-start.11
  (354 other events, 664.6 us)
Sparse Core Ops, SparseCore 0:
  678.3 129.5 all-reduce.53
where the time goes:
time: 827 us; the launch traced here: 817 us
  local copies, waits for them, and re-layouts  424 us (51%)
  other arithmetic  151 us (18%)
  matrix products  85.6 us (10%)
  waiting for transfers between devices  85.1 us (10%)
  blocking collectives  49.3 us (6%)
  between operations  14.1 us (2%)
    concatenate x104, local copies, waits for them, and re-layouts, make_patches(): stacked = jnp.concatenate(taps, axis=3)  192 us
    slice x40, local copies, waits for them, and re-layouts, make_patches(): padded[:, a:a + side, e:e + side, :]  115 us
    psum x1, waiting for transfers between devices, per_device(): summed = lax.psum(conv_grad, ('dp', 'section'))  85.1 us
    while x800, local copies, waits for them, and re-layouts  72.5 us
    convert_element_type x40, other arithmetic, block_forward(): swish(skip + respond(pre_second, gains[1], biases[1], count))  48.6 us
    psum x1, blocking collectives, per_device(): lax.psum((norm_grad, head_w_grad, head_b_grad), ('dp', 'section'))  40.8 us
    convert_element_type x72, other arithmetic, block_forward(): swish(respond(pre_first, gains[0], biases[0], count)).astype(jnp.bfloat16)  37.2 us
    reduce_sum x48, other arithmetic, respond(): return (gain * normed + bias).reshape(values.shape)  36.8 us
  transfers between devices with their start and end apart: 1, of which 1 were waited for; matrix products, arithmetic and copies ran while one was open for 0% of the time, Pallas kernels for 0%

commit v1 on v0

v1 whole, which is shorter than its diff:
```python
import functools

import jax
import jax.numpy as jnp
from jax import lax
from jax.experimental import pallas as pl
from jax.experimental.pallas import tpu as pltpu
from jax.sharding import PartitionSpec as P

F32 = jnp.float32
BF16 = jnp.bfloat16
eps = 1e-06
prior_precision = 0.5
OFFSETS = (0, 1, 2, -1)


def kernel(total, img, labels, wt, gain, bias, hw, hb, big, small,
           xs, zs, dsw, rs, wf, wb, qs, qt, du2, du1, hw2, lab):
    lane = lax.broadcasted_iota(jnp.int32, (1, 128), 1)
    low = lane < 64

    def both(v):
        return v + pltpu.roll(v, 64, 1)

    def twice(v):
        return jnp.concatenate([v, v], axis=1)

    for ref in (qs, qt):
        ref[0] = jnp.zeros(ref.shape[1:], BF16)
        ref[9] = jnp.zeros(ref.shape[1:], BF16)
    for k in range(6):
        xs[k, 0] = jnp.zeros((256, 256), BF16)
        xs[k, 9] = jnp.zeros((256, 256), BF16)

    def spread(b, carry):
        flat = wt[b].astype(F32)
        zero = jnp.zeros((64, 128), BF16)
        cols = jnp.concatenate([flat, jnp.zeros((128, 64), F32)], axis=1).T
        plain = [cols[t * 64:(t + 1) * 64] for t in range(9)]
        turned = [pltpu.roll(v, 64, 1) for v in plain]
        none = jnp.zeros((64, 128), F32)
        for j in range(2):
            first, second = (plain, turned) if j == 0 else (turned, plain)
            for a in range(3):
                for s, xi in enumerate(OFFSETS):
                    left = first[a * 3 + xi + 1] if 0 <= xi + 1 <= 2 else none
                    right = second[a * 3 + xi] if 0 <= xi <= 2 else none
                    tile = jnp.where(low, left, right).astype(BF16)
                    for yo in range(2):
                        row = (a + yo) * 256 + s * 64
                        wf[2 * b + j, row:row + 64, yo * 128:yo * 128 + 128] = tile
        wide = jnp.concatenate(
            [jnp.zeros((128, 64), F32), flat, jnp.zeros((128, 128), F32)], axis=1)
        for a in range(3):
            for s, xi in enumerate(OFFSETS):
                at = ((2 - a) * 3 + 2 - xi) * 64
                tile = wide[:, at:at + 128]
                if xi == -1:
                    tile = jnp.where(low, tile, 0.0)
                if xi == 2:
                    tile = jnp.where(low, 0.0, tile)
                tile = tile.astype(BF16)
                for j in range(2):
                    for yo in range(2):
                        row = (a + yo) * 256 + s * 64
                        wb[2 * b + j, row:row + 64, yo * 128:yo * 128 + 128] = (
                            tile[j * 64:j * 64 + 64])
        for j in range(2):
            for ref in (wf, wb):
                for s in range(4):
                    ref[2 * b + j, 768 + s * 64:832 + s * 64, 0:128] = zero
                    ref[2 * b + j, s * 64:s * 64 + 64, 128:256] = zero
        return carry

    lax.fori_loop(0, 3, spread, 0)

    def put(ref, y, v):
        edge = jnp.zeros((1, 64, 128), F32)
        after = jnp.concatenate([v[1:], edge], axis=0)
        before = jnp.concatenate([edge, v[:3]], axis=0)
        beside = jnp.where(low[None], after, before)
        ref[y + 1, :, 0:128] = v.reshape(256, 128).astype(BF16)
        ref[y + 1, :, 128:256] = beside.reshape(256, 128).astype(BF16)

    def conv(src, w, body, init):
        def step(y2, carry):
            rows = jnp.concatenate([src[2 * y2 + r] for r in range(4)], axis=1)
            out = jnp.dot(rows, w[...], preferred_element_type=F32)
            for yo in range(2):
                carry = body(2 * y2 + yo, out[:, yo * 128:yo * 128 + 128], carry)
            return carry
        return lax.fori_loop(0, 4, step, init)

    zero_sum = jnp.zeros((64, 128), F32)

    def over_pairs(v):
        return jnp.sum(v.reshape(4, 64, 128), axis=0)

    for y in range(8):
        slab = jnp.stack([img[:, (y * 4 + j) * 128:(y * 4 + j + 1) * 128]
                          for j in range(4)], axis=0).astype(F32)
        put(xs.at[0], y, slab)

    pooled = zero_sum
    for k in range(6):
        b, j = k // 2, k % 2

        def keep(y, out, energy):
            zs[k, y] = out
            return energy + over_pairs(out * out)

        energy = conv(xs.at[k], wf.at[k], keep, zero_sum)
        r = lax.rsqrt(both(energy) * (1.0 / 64) + eps)
        rs[k] = r
        scale = r * twice(gain[b, j:j + 1, :])
        shift = twice(bias[b, j:j + 1, :])

        def activate(y, carry):
            u = zs[k, y].reshape(4, 64, 128) * scale[None] + shift[None]
            if j == 1:
                u = u + xs[k - 1, y + 1, :, 0:128].astype(F32).reshape(4, 64, 128)
            sig = 0.5 * jnp.tanh(0.5 * u) + 0.5
            out = u * sig
            dsw[k, y] = (sig + out * (1.0 - sig)).reshape(256, 128)
            if k < 5:
                put(xs.at[k + 1], y, out)
                return carry
            return carry + jnp.sum(out.astype(BF16).astype(F32), axis=0)

        pooled = lax.fori_loop(0, 8, activate, pooled)

    pooled = both(pooled) * (1.0 / 64)
    hw2[...] = jnp.zeros((128, 128), F32)
    hw2[0:64, 0:hw.shape[1]] = hw[...]
    hw2[64:128, 0:hw.shape[1]] = hw[...]
    lab[...] = jnp.zeros((8, 128), jnp.int32)
    lab[0:1, 0:64] = labels[...]
    classes = hw.shape[1]
    hbias = jnp.concatenate([hb[...], jnp.zeros((1, 128 - classes), F32)], axis=1)
    logits = jnp.dot(jnp.where(low, pooled, 0.0), hw2[...],
                     precision=lax.Precision.HIGHEST, preferred_element_type=F32) + hbias
    live = lane < classes
    logits = jnp.where(live, logits, -1e30)
    top = jnp.max(logits, axis=1, keepdims=True)
    expo = jnp.where(live, jnp.exp(logits - top), 0.0)
    probs = expo / jnp.sum(expo, axis=1, keepdims=True)
    onehot = jnp.where(
        lax.broadcasted_iota(jnp.int32, (128, 128), 0) == lab[0:1, :], 1.0, 0.0).T
    dl = (probs - onehot[0:64]) * (1.0 / total)
    dlt = jnp.concatenate([dl, jnp.zeros((64, 128), F32)], axis=0).T
    tall = jnp.concatenate([pooled, jnp.zeros((64, 128), F32)], axis=0)
    small[...] = jnp.zeros((32, 128), F32)
    small[16:32, :] = jnp.dot(dlt[0:16], tall, precision=lax.Precision.HIGHEST,
                              preferred_element_type=F32)
    small[12:13, :] = jnp.sum(dl, axis=0, keepdims=True)
    spread_g = lax.dot_general(dl, hw2[...], (((1,), (1,)), ((), ())),
                               precision=lax.Precision.HIGHEST,
                               preferred_element_type=F32) * (1.0 / 64)
    spread_g = spread_g.astype(BF16).astype(F32)

    def tally(k, y, d, sums):
        return (sums[0] + over_pairs(d * zs[k, y]), sums[1] + over_pairs(d))

    def begin(y, sums):
        d = (dsw[5, y].reshape(4, 64, 128) * spread_g[None]).reshape(256, 128)
        du2[y] = d
        return tally(5, y, d, sums)

    sums = lax.fori_loop(0, 8, begin, (zero_sum, zero_sum))
    for k in range(5, -1, -1):
        b, j = k // 2, k % 2
        source = du2 if j == 1 else du1
        r = rs[k]
        dg = both(sums[0]) * r
        db = both(sums[1])
        small[2 * k:2 * k + 1, :] = jnp.sum(dg, axis=0, keepdims=True)
        small[2 * k + 1:2 * k + 2, :] = jnp.sum(db, axis=0, keepdims=True)
        c1 = r * twice(gain[b, j:j + 1, :])
        c2 = c1 * dg * r * (1.0 / 64)

        def settle(y, carry):
            d = (source[y].reshape(4, 64, 128) * c1[None]
                 - zs[k, y].reshape(4, 64, 128) * c2[None])
            if k > 0:
                put(qs, y, d)
            qt[y + 1] = d.reshape(256, 128).T.astype(BF16)
            return carry

        lax.fori_loop(0, 8, settle, 0)

        left = jnp.concatenate(
            [jnp.concatenate([qt[y - a + 2] for y in range(8)], axis=1) for a in range(3)],
            axis=0)
        right = jnp.concatenate([xs[k, y + 1] for y in range(8)], axis=0)
        terms = jnp.dot(left, right, preferred_element_type=F32)
        parts = []
        for a in range(3):
            zero_side = pltpu.roll(terms[a * 128:a * 128 + 64], 64, 1)
            parts.append((zero_side + terms[a * 128 + 64:a * 128 + 128])[:, 0:192])
        big[k] = jnp.concatenate(parts, axis=1)

        if j == 1:
            def to_first(y, out, sums):
                d = out * dsw[k - 1, y]
                du1[y] = d
                return tally(k - 1, y, d, sums)

            sums = conv(qs, wb.at[k], to_first, (zero_sum, zero_sum))
        elif k > 0:
            def to_second(y, out, sums):
                g = (du2[y] + out).astype(BF16).astype(F32)
                d = g * dsw[k - 1, y]
                du2[y] = d
                return tally(k - 1, y, d, sums)

            sums = conv(qs, wb.at[k], to_second, (zero_sum, zero_sum))


def local_grads(total, images_in, labels, wt, gain, bias, hw, hb, interpret=False):
    vmem = pl.BlockSpec(memory_space=pltpu.VMEM)
    return pl.pallas_call(
        functools.partial(kernel, total),
        out_shape=(jax.ShapeDtypeStruct((6, 64, 576), F32),
                   jax.ShapeDtypeStruct((32, 128), F32)),
        in_specs=[vmem] * 7,
        out_specs=(vmem, vmem),
        scratch_shapes=[
            pltpu.VMEM((6, 10, 256, 256), BF16),
            pltpu.VMEM((6, 8, 256, 128), F32),
            pltpu.VMEM((6, 8, 256, 128), F32),
            pltpu.VMEM((6, 64, 128), F32),
            pltpu.VMEM((6, 1024, 256), BF16),
            pltpu.VMEM((6, 1024, 256), BF16),
            pltpu.VMEM((10, 256, 256), BF16),
            pltpu.VMEM((10, 128, 256), BF16),
            pltpu.VMEM((8, 256, 128), F32),
            pltpu.VMEM((8, 256, 128), F32),
            pltpu.VMEM((128, 128), F32),
            pltpu.VMEM((8, 128), jnp.int32),
        ],
        compiler_params=pltpu.CompilerParams(vmem_limit_bytes=52 * 1024 * 1024),
        interpret=interpret,
    )(images_in, labels, wt, gain, bias, hw, hb)


def per_device(images_in, labels, conv_weight, frn_gain, frn_bias, head_weight, head_bias):
    images = images_in.shape[0]
    total = images * lax.axis_size("dp") * lax.axis_size("section")
    share = jnp.swapaxes(conv_weight.astype(BF16), 2, 3)
    wt = lax.all_gather(share, "section", axis=2, tiled=True).reshape(3, 128, 576)
    big, small = local_grads(total, images_in, labels.reshape(1, images), wt, frn_gain,
                             frn_bias, head_weight, head_bias.reshape(1, -1))
    owned = lax.psum_scatter(big, "section", scatter_dimension=1, tiled=True)
    owned = lax.psum(owned, "dp")
    small = lax.psum(small, ("dp", "section"))
    classes = head_bias.shape[0]
    params = jnp.stack([frn_gain, frn_bias], axis=2)
    return (
        jnp.swapaxes(owned, 1, 2).reshape(conv_weight.shape) + prior_precision * conv_weight,
        small[0:12, 0:64].reshape(params.shape) + prior_precision * params,
        small[16:16 + classes, 0:64].T + prior_precision * head_weight,
        small[12, 0:classes] + prior_precision * head_bias,
    )


def solution(mesh):
    return jax.shard_map(
        per_device,
        mesh=mesh,
        in_specs=(
            P(("dp", "section"), None),
            P(("dp", "section")),
            P(None, None, None, "section"),
            P(),
            P(),
            P(),
            P(),
        ),
        out_specs=(P(None, None, None, "section"), P(), P(), P()),
        check_vma=False,
    )
```

time: 827 us -> 170 us (0.21); the launches traced: 817 us -> 170 us
  local copies, waits for them, and re-layouts: 424 us -> 1.54 us
  other arithmetic: 151 us -> 4.37 us
  matrix products: 85.6 us -> 0 us
  Pallas kernels: 0 us -> 30.5 us
  waiting for transfers between devices: 85.1 us -> 70.4 us
    concatenate x104 -> x0, local copies, waits for them, and re-layouts: 192 us -> none  [make_patches(): stacked = jnp.concatenate(taps, axis=3)]
    slice x40 -> x1, local copies, waits for them, and re-layouts: 115 us -> 0.01 us  [per_device(): small[0:12, 0:64].reshape(params.shape) + prior_precision * params]
    convert_element_type x161 -> x0, other arithmetic: 91 us -> none  [the longest x40 48.6 us: block_forward(): swish(skip + respond(pre_second, gains[1], biases[1], count))]
    dot_general x160 -> x0, matrix products: 85.6 us -> none  [the longest x24 24.5 us: block_forward(): jnp.dot(cols_second, w_second, preferred_element_type=jnp.float32)]
    while x800 -> x0, local copies, waits for them, and re-layouts: 72.5 us -> none
    reduce_sum x72 -> x0, other arithmetic: 44.9 us -> none  [the longest x48 36.8 us: respond(): return (gain * normed + bias).reshape(values.shape)]
    pallas_call x0 -> x1, Pallas kernels: none -> 30.5 us  [local_grads(): pl.pallas_call(functools.partial(kernel, total), out_shape=(jax.ShapeDtyp...]
    split x40 -> x0, local copies, waits for them, and re-layouts: 15.5 us -> none  [make_patches(): stacked = jnp.concatenate(taps, axis=3)]
  transfers between devices with their start and end apart: 1 -> 2, of which waited for: 1 -> 1; matrix products, arithmetic and copies ran while one was open for 0% -> 1% of each run, Pallas kernels for 0% -> 0%
where the time goes in v1:
time: 170 us
  waiting for transfers between devices  70.4 us (41%)
  blocking collectives  48.7 us (29%)
  Pallas kernels  30.5 us (18%)
  between operations  14.1 us (8%)
  other arithmetic  4.37 us (3%)
    psum x1, waiting for transfers between devices, per_device(): owned = lax.psum(owned, 'dp')  70.4 us
    psum x1, blocking collectives, per_device(): small = lax.psum(small, ('dp', 'section'))  40.2 us
    pallas_call x1, Pallas kernels, local_grads(): pl.pallas_call(functools.partial(kernel, total), out_shape=(jax.ShapeDtyp...  30.5 us
    all_gather x1, blocking collectives, per_device(): lax.all_gather(share, 'section', axis=2, tiled=True).reshape(3, 128, 576)  8.47 us
  transfers between devices with their start and end apart: 2, of which 1 were waited for; matrix products, arithmetic and copies ran while one was open for 1% of the time, Pallas kernels for 0%

profile of v1, /device:TPU:0, one launch (start us, length us, event | category | flops | bytes accessed | tf_op | source)
XLA Modules:
  0.0 169.7 jit_solution(11466445799969574639)
XLA Ops:
  7.2 0.0 copy-start
  7.2 0.0 reduce-scatter.2.cloned.1.call-start
  7.2 0.8 copy.11.hw
  8.1 1.0 convert_bitcast_fusion
  9.0 0.0 copy-start.2
  9.0 8.5 %all_gather.3 = bf16[3,2,64,576]{3,2,1,0:T(8,128)(2,1)S(1)} all-gather(bf16[3,2,16,576]{3,2,1,0:T(8,128)(2,1)S(1)} %convert_bitcast_fusion), channel_id=1, replica_groups=mesh['dp'=8,'section'=4] {'section'}, dimensions={2}, use_global_device_ids=true | all-gather | bytes 552960 | tf_op jit(solution)/shard_map/all_gather | solution.py:250
  17.5 0.0 copy-start.1
  17.5 0.0 copy-start.3
  17.5 0.0 copy-start.4
  17.5 0.0 copy-done
  17.5 0.0 copy-done.2
  17.5 0.7 copy-done.1
  18.2 0.0 copy-done.3
  18.2 0.0 copy-done.4
  18.2 30.5 %shard_map.102 = (f32[6,64,576]{2,1,0:T(8,128)}, f32[32,128]{1,0:T(8,128)S(1)}) custom-call(bf16[64,4096]{1,0:T(8,128)(2,1)S(1)} %copy-done, s32[1,64]{1,0:T(1,128)S(1)} %bitcast.21, bf16[3,128,576]{2,1,0:T(8,128)(2,1)S(1)} %bitcast.18, f32[3,2,64]{2,1,0:T(2,128)S(1)} %copy-done.1, f32[3,2,64]{2,1,0:T(2,128)S(1)} %copy-done.2, f32[64,10]{1,0:T(8,128)S(1)} %copy.11.hw, ...), custom_call_target="tpu_custom_call" | custom-call | tf_op jit(solution)/shard_map/pallas_call | solution.py:221
  48.7 0.0 copy-start.6
  48.7 0.0 reduce-scatter.2.cloned.1.call-update
  48.8 0.0 copy-start.5
  48.8 0.0 all-reduce.2.cloned.1.call-start
  48.8 40.2 %psum.15 = f32[32,128]{1,0:T(8,128)S(1)} all-reduce(f32[32,128]{1,0:T(8,128)S(1)} %get-tuple-element.7), channel_id=1, replica_groups=mesh['dp'=8,'section'=4] {'dp','section'}, use_global_device_ids=true, to_apply=%region_2.0 | all-reduce | flops 4096 | bytes 32768 | tf_op jit(solution)/shard_map/psum | solution.py:255
  89.1 0.6 fusion.1
  89.7 0.0 copy-done.6
  89.7 0.6 fusion
  90.3 0.0 reduce-scatter.2.cloned.1.call-done
  90.3 0.0 all-reduce.2.cloned.1.call-update
  90.3 0.5 fusion.2
  90.8 70.4 %all-reduce.2.cloned.1.call-done = f32[3,2,576,16]{2,3,1,0:T(8,128)} async-done(((f32[3,2,576,16]{2,3,1,0:T(8,128)}), f32[3,2,576,16]{2,3,1,0:T(8,128)}) %all-reduce.2.cloned.1.call-update) | async-done | bytes 221200 | tf_op jit(solution)/shard_map/psum | solution.py:254
  161.2 0.0 copy-done.5
  161.2 1.7 multiply_add_fusion
  (2 shorter events, 0.0 us)
Async XLA Ops:
  7.2 10.3 %copy-start = (bf16[64,4096]{1,0:T(8,128)(2,1)S(1)}, bf16[64,4096]{1,0:T(8,128)(2,1)}, u32[]{:S(2)}) copy-start(bf16[64,4096]{1,0:T(8,128)(2,1)} %img.1) | copy-start | bytes 1572868
  7.2 83.1 %reduce-scatter.2.cloned.1.call-start = ((), (), s32[]{:S(2)}) async-start(), calls=%async_computation.1 | async-start | bytes 1228800 | tf_op jit(solution)/shard_map/reduce_scatter | solution.py:253
  9.0 8.5 %copy-start.2 = (f32[3,2,64]{2,1,0:T(2,128)S(1)}, f32[3,2,64]{2,1,0:T(2,128)}, u32[]{:S(2)}) copy-start(f32[3,2,64]{2,1,0:T(2,128)} %bias.1) | copy-start | bytes 4612
  17.5 0.7 copy-start.1
  17.5 0.7 copy-start.3
  17.5 0.7 copy-start.4
  48.7 41.0 %copy-start.6 = (f32[64,10]{0,1:T(8,128)S(1)}, f32[64,10]{0,1:T(8,128)}, u32[]{:S(2)}) copy-start(f32[64,10]{0,1:T(8,128)} %param.12) | copy-start | bytes 7684
  48.8 112.4 %copy-start.5 = (f32[3,2,576,16]{2,3,1,0:T(8,128)S(1)}, f32[3,2,576,16]{2,3,1,0:T(8,128)}, u32[]{:S(2)}) copy-start(f32[3,2,576,16]{2,3,1,0:T(8,128)} %param.9) | copy-start | bytes 663556
  48.8 112.4 %all-reduce.2.cloned.1.call-start = ((), (), s32[]{:S(2)}) async-start(), calls=%async_computation.2 | async-start | bytes 491520 | tf_op jit(solution)/shard_map/psum | solution.py:254
Sparse Core Ops, SparseCore 0:
  48.9 25.3 reduce-scatter.1
  90.4 70.7 all-reduce.1

commit v2 on v1

--- a/solution.py
+++ b/solution.py
@@ -9,13 +9,92 @@
 
 F32 = jnp.float32
 BF16 = jnp.bfloat16
+MESH = pl.DeviceIdType.MESH
 eps = 1e-06
 prior_precision = 0.5
 OFFSETS = (0, 1, 2, -1)
 
 
-def kernel(total, img, labels, wt, gain, bias, hw, hb, big, small,
-           xs, zs, dsw, rs, wf, wb, qs, qt, du2, du1, hw2, lab):
+def kernel(total, dps, secs, img, labels, own, gain, bias, hw, hb, conv_out, small,
+           xs, zs, dsw, rs, wf, wb, qs, qt, du2, du1, hw2, lab, wt, buf, in_a, tot, in_b,
+           fin, w_send, w_recv, a_send, a_recv, b_send, b_recv, c_send, c_recv):
+    dp, sec = lax.axis_index("dp"), lax.axis_index("section")
+    tiles = in_a.shape[2]
+    per = in_b.shape[2]
+
+    barrier = pltpu.get_barrier_semaphore()
+    for d in range(1, secs):
+        pl.semaphore_signal(barrier, inc=1, device_id=(dp, lax.rem(sec + d, secs)),
+                            device_id_type=MESH)
+
+    def greet(d, carry):
+        pl.semaphore_signal(barrier, inc=1, device_id=(lax.rem(dp + d, dps), sec),
+                            device_id_type=MESH)
+        return carry
+
+    lax.fori_loop(1, dps, greet, 0)
+    wt[sec] = own[...].astype(BF16)
+    pl.semaphore_wait(barrier, secs - 1 + dps - 1)
+
+    def send_w(d):
+        return pltpu.make_async_remote_copy(
+            src_ref=wt.at[sec], dst_ref=wt.at[sec], send_sem=w_send.at[d - 1],
+            recv_sem=w_recv.at[d - 1], device_id=(dp, lax.rem(sec + d, secs)),
+            device_id_type=MESH)
+
+    def send_a(b, d):
+        to = lax.rem(sec + d, secs)
+        return pltpu.make_async_remote_copy(
+            src_ref=buf.at[b, to], dst_ref=in_a.at[b, d - 1], send_sem=a_send.at[b, d - 1],
+            recv_sem=a_recv.at[b, d - 1], device_id=(dp, to), device_id_type=MESH)
+
+    def send_b(b, d):
+        to = lax.rem(dp + d, dps)
+        return pltpu.make_async_remote_copy(
+            src_ref=tot.at[b, pl.ds(to * per, per)], dst_ref=in_b.at[b, d - 1],
+            send_sem=b_send.at[b, d - 1], recv_sem=b_recv.at[b, d - 1],
+            device_id=(to, sec), device_id_type=MESH)
+
+    def send_c(b, d):
+        to = lax.rem(dp + d, dps)
+        mine = fin.at[b, pl.ds(dp * per, per)]
+        return pltpu.make_async_remote_copy(
+            src_ref=mine, dst_ref=mine, send_sem=c_send.at[b, d - 1],
+            recv_sem=c_recv.at[b, d - 1], device_id=(to, sec), device_id_type=MESH)
+
+    def each_dp(act):
+        def step(d, carry):
+            act(d)
+            return carry
+        lax.fori_loop(1, dps, step, 0)
+
+    def start_a(b):
+        for d in range(1, secs):
+            send_a(b, d).start()
+
+    def start_b(b):
+        for d in range(1, secs):
+            send_a(b, d).wait_recv()
+        all_terms = buf[b, sec]
+        for d in range(1, secs):
+            all_terms = all_terms + in_a[b, d - 1]
+        tot[b, 0:tiles] = all_terms
+        if tot.shape[1] > tiles:
+            tot[b, tiles:] = jnp.zeros((tot.shape[1] - tiles, 8, 128), F32)
+        each_dp(lambda d: send_b(b, d).start())
+
+    def start_c(b):
+        each_dp(lambda d: send_b(b, d).wait_recv())
+        sums = lax.fori_loop(1, dps, lambda d, acc: acc + in_b[b, d - 1],
+                             tot[b, pl.ds(dp * per, per)])
+        fin[b, pl.ds(dp * per, per)] = sums
+        each_dp(lambda d: send_c(b, d).start())
+
+    def end_c(b):
+        each_dp(lambda d: send_c(b, d).wait_recv())
+
+    for d in range(1, secs):
+        send_w(d).start()
     lane = lax.broadcasted_iota(jnp.int32, (1, 128), 1)
     low = lane < 64
 
@@ -32,8 +111,39 @@
         xs[k, 0] = jnp.zeros((256, 256), BF16)
         xs[k, 9] = jnp.zeros((256, 256), BF16)
 
+    def put(ref, y, v):
+        edge = jnp.zeros((1, 64, 128), F32)
+        after = jnp.concatenate([v[1:], edge], axis=0)
+        before = jnp.concatenate([edge, v[:3]], axis=0)
+        beside = jnp.where(low[None], after, before)
+        ref[y + 1, :, 0:128] = v.reshape(256, 128).astype(BF16)
+        ref[y + 1, :, 128:256] = beside.reshape(256, 128).astype(BF16)
+
+    def conv(src, w, body, init):
+        def step(y2, carry):
+            rows = jnp.concatenate([src[2 * y2 + r] for r in range(4)], axis=1)
+            out = jnp.dot(rows, w[...], preferred_element_type=F32)
+            for yo in range(2):
+                carry = body(2 * y2 + yo, out[:, yo * 128:yo * 128 + 128], carry)
+            return carry
+        return lax.fori_loop(0, 4, step, init)
+
+    zero_sum = jnp.zeros((64, 128), F32)
+
+    def over_pairs(v):
+        return jnp.sum(v.reshape(4, 64, 128), axis=0)
+
+    for y in range(8):
+        slab = jnp.stack([img[:, (y * 4 + j) * 128:(y * 4 + j + 1) * 128]
+                          for j in range(4)], axis=0).astype(F32)
+        put(xs.at[0], y, slab)
+
+    for d in range(1, secs):
+        send_w(d).wait_recv()
+
     def spread(b, carry):
-        flat = wt[b].astype(F32)
+        flat = jnp.concatenate(
+            [wt[q, 2 * b + j] for j in range(2) for q in range(secs)], axis=0).astype(F32)
         zero = jnp.zeros((64, 128), BF16)
         cols = jnp.concatenate([flat, jnp.zeros((128, 64), F32)], axis=1).T
         plain = [cols[t * 64:(t + 1) * 64] for t in range(9)]
@@ -74,33 +184,6 @@
 
     lax.fori_loop(0, 3, spread, 0)
 
-    def put(ref, y, v):
-        edge = jnp.zeros((1, 64, 128), F32)
-        after = jnp.concatenate([v[1:], edge], axis=0)
-        before = jnp.concatenate([edge, v[:3]], axis=0)
-        beside = jnp.where(low[None], after, before)
-        ref[y + 1, :, 0:128] = v.reshape(256, 128).astype(BF16)
-        ref[y + 1, :, 128:256] = beside.reshape(256, 128).astype(BF16)
-
-    def conv(src, w, body, init):
-        def step(y2, carry):
-            rows = jnp.concatenate([src[2 * y2 + r] for r in range(4)], axis=1)
-            out = jnp.dot(rows, w[...], preferred_element_type=F32)
-            for yo in range(2):
-                carry = body(2 * y2 + yo, out[:, yo * 128:yo * 128 + 128], carry)
-            return carry
-        return lax.fori_loop(0, 4, step, init)
-
-    zero_sum = jnp.zeros((64, 128), F32)
-
-    def over_pairs(v):
-        return jnp.sum(v.reshape(4, 64, 128), axis=0)
-
-    for y in range(8):
-        slab = jnp.stack([img[:, (y * 4 + j) * 128:(y * 4 + j + 1) * 128]
-                          for j in range(4)], axis=0).astype(F32)
-        put(xs.at[0], y, slab)
-
     pooled = zero_sum
     for k in range(6):
         b, j = k // 2, k % 2
@@ -149,10 +232,14 @@
     dl = (probs - onehot[0:64]) * (1.0 / total)
     dlt = jnp.concatenate([dl, jnp.zeros((64, 128), F32)], axis=0).T
     tall = jnp.concatenate([pooled, jnp.zeros((64, 128), F32)], axis=0)
-    small[...] = jnp.zeros((32, 128), F32)
-    small[16:32, :] = jnp.dot(dlt[0:16], tall, precision=lax.Precision.HIGHEST,
-                              preferred_element_type=F32)
-    small[12:13, :] = jnp.sum(dl, axis=0, keepdims=True)
+    d_head = jnp.dot(dlt[0:16], tall, precision=lax.Precision.HIGHEST,
+                     preferred_element_type=F32)
+    row = lax.broadcasted_iota(jnp.int32, (8, 128), 0)
+    extra = jnp.where(row == 4, jnp.sum(dl, axis=0, keepdims=True), 0.0)
+    for q in range(secs):
+        for b in range(3):
+            buf[b, q, 19] = d_head[0:8] if b == 2 else jnp.zeros((8, 128), F32)
+            buf[b, q, 20] = d_head[8:16] if b == 2 else jnp.zeros((8, 128), F32)
     spread_g = lax.dot_general(dl, hw2[...], (((1,), (1,)), ((), ())),
                                precision=lax.Precision.HIGHEST,
                                preferred_element_type=F32) * (1.0 / 64)
@@ -173,8 +260,11 @@
         r = rs[k]
         dg = both(sums[0]) * r
         db = both(sums[1])
-        small[2 * k:2 * k + 1, :] = jnp.sum(dg, axis=0, keepdims=True)
-        small[2 * k + 1:2 * k + 2, :] = jnp.sum(db, axis=0, keepdims=True)
+        extra = jnp.where(row == 2 * j, jnp.sum(dg, axis=0, keepdims=True), extra)
+        extra = jnp.where(row == 2 * j + 1, jnp.sum(db, axis=0, keepdims=True), extra)
+        if j == 0:
+            for q in range(secs):
+                buf[b, q, 18] = extra
         c1 = r * twice(gain[b, j:j + 1, :])
         c2 = c1 * dg * r * (1.0 / 64)
 
@@ -193,11 +283,24 @@
             axis=0)
         right = jnp.concatenate([xs[k, y + 1] for y in range(8)], axis=0)
         terms = jnp.dot(left, right, preferred_element_type=F32)
-        parts = []
         for a in range(3):
             zero_side = pltpu.roll(terms[a * 128:a * 128 + 64], 64, 1)
-            parts.append((zero_side + terms[a * 128 + 64:a * 128 + 128])[:, 0:192])
-        big[k] = jnp.concatenate(parts, axis=1)
+            both_sides = zero_side + terms[a * 128 + 64:a * 128 + 128]
+            for e in range(3):
+                at = e // 2 * 128
+                here = both_sides[:, at:at + 128]
+                there = pltpu.roll(here, 64, 1)
+                first, second = (here, there) if e % 2 == 0 else (there, here)
+                for q in range(secs):
+                    buf[b, q, j * 9 + a * 3 + e] = jnp.where(
+                        low, first[q * 16:q * 16 + 8], second[q * 16 + 8:q * 16 + 16])
+
+        if j == 0:
+            start_a(b)
+        if k <= 3 and j == 1:
+            start_b(b + 1)
+        if k <= 2 and j == 0:
+            start_c(b + 1)
 
         if j == 1:
             def to_first(y, out, sums):
@@ -215,13 +318,36 @@
 
             sums = conv(qs, wb.at[k], to_second, (zero_sum, zero_sum))
 
-
-def local_grads(total, images_in, labels, wt, gain, bias, hw, hb, interpret=False):
+    start_b(0)
+    start_c(0)
+    for b in (2, 1, 0):
+        end_c(b)
+    for b in range(3):
+        for j in range(2):
+            rows = [fin[b, j * 9 + t] for t in range(9)]
+            conv_out[2 * b + j, 0:8] = jnp.concatenate([v[:, 0:64] for v in rows], axis=1)
+            conv_out[2 * b + j, 8:16] = jnp.concatenate([v[:, 64:128] for v in rows], axis=1)
+        small[b * 8:b * 8 + 8] = fin[b, 18]
+    small[24:32] = fin[2, 19]
+    small[32:40] = fin[2, 20]
+    for d in range(1, secs):
+        send_w(d).wait_send()
+    for b in range(3):
+        for d in range(1, secs):
+            send_a(b, d).wait_send()
+        each_dp(lambda d: send_b(b, d).wait_send())
+        each_dp(lambda d: send_c(b, d).wait_send())
+
+
+def all_grads(total, dps, secs, images_in, labels, own, gain, bias, hw, hb):
     vmem = pl.BlockSpec(memory_space=pltpu.VMEM)
+    tiles = 21
+    per = -(-tiles // dps)
+    dma = pltpu.SemaphoreType.DMA
     return pl.pallas_call(
-        functools.partial(kernel, total),
-        out_shape=(jax.ShapeDtypeStruct((6, 64, 576), F32),
-                   jax.ShapeDtypeStruct((32, 128), F32)),
+        functools.partial(kernel, total, dps, secs),
+        out_shape=(jax.ShapeDtypeStruct(own.shape, F32),
+                   jax.ShapeDtypeStruct((40, 128), F32)),
         in_specs=[vmem] * 7,
         out_specs=(vmem, vmem),
         scratch_shapes=[
@@ -237,29 +363,39 @@
             pltpu.VMEM((8, 256, 128), F32),
             pltpu.VMEM((128, 128), F32),
             pltpu.VMEM((8, 128), jnp.int32),
+            pltpu.VMEM((secs,) + own.shape, BF16),
+            pltpu.VMEM((3, secs, tiles, 8, 128), F32),
+            pltpu.VMEM((3, secs - 1, tiles, 8, 128), F32),
+            pltpu.VMEM((3, per * dps, 8, 128), F32),
+            pltpu.VMEM((3, dps - 1, per, 8, 128), F32),
+            pltpu.VMEM((3, per * dps, 8, 128), F32),
+            dma((secs - 1,)), dma((secs - 1,)),
+            dma((3, secs - 1)), dma((3, secs - 1)),
+            dma((3, dps - 1)), dma((3, dps - 1)),
+            dma((3, dps - 1)), dma((3, dps - 1)),
         ],
-        compiler_params=pltpu.CompilerParams(vmem_limit_bytes=52 * 1024 * 1024),
-        interpret=interpret,
-    )(images_in, labels, wt, gain, bias, hw, hb)
+        compiler_params=pltpu.CompilerParams(
+            vmem_limit_bytes=52 * 1024 * 1024, collective_id=0, has_side_effects=True),
+    )(images_in, labels, own, gain, bias, hw, hb)
 
 
 def per_device(images_in, labels, conv_weight, frn_gain, frn_bias, head_weight, head_bias):
     images = images_in.shape[0]
-    total = images * lax.axis_size("dp") * lax.axis_size("section")
-    share = jnp.swapaxes(conv_weight.astype(BF16), 2, 3)
-    wt = lax.all_gather(share, "section", axis=2, tiled=True).reshape(3, 128, 576)
-    big, small = local_grads(total, images_in, labels.reshape(1, images), wt, frn_gain,
+    dps, secs = lax.axis_size("dp"), lax.axis_size("section")
+    blocks, convs, depth, share = conv_weight.shape
+    own = jnp.swapaxes(conv_weight, 2, 3).reshape(blocks * convs, share, depth)
+    owned, small = all_grads(images * dps * secs, dps, secs, images_in,
+                             labels.reshape(1, images), own, frn_gain,
                              frn_bias, head_weight, head_bias.reshape(1, -1))
-    owned = lax.psum_scatter(big, "section", scatter_dimension=1, tiled=True)
-    owned = lax.psum(owned, "dp")
-    small = lax.psum(small, ("dp", "section"))
     classes = head_bias.shape[0]
     params = jnp.stack([frn_gain, frn_bias], axis=2)
     return (
-        jnp.swapaxes(owned, 1, 2).reshape(conv_weight.shape) + prior_precision * conv_weight,
-        small[0:12, 0:64].reshape(params.shape) + prior_precision * params,
-        small[16:16 + classes, 0:64].T + prior_precision * head_weight,
-        small[12, 0:classes] + prior_precision * head_bias,
+        jnp.swapaxes(owned.reshape(blocks, convs, share, depth), 2, 3)
+        + prior_precision * conv_weight,
+        small[0:24].reshape(3, 8, 128)[:, 0:4, 0:64].reshape(params.shape)
+        + prior_precision * params,
+        small[24:24 + classes, 0:64].T + prior_precision * head_weight,
+        small[20, 0:classes] + prior_precision * head_bias,
     )
 
 

time: 170 us -> 67.7 us (0.40)
  waiting for transfers between devices: 70.4 us -> 0 us
  blocking collectives: 48.7 us -> 0 us
  Pallas kernels: 30.5 us -> 60.7 us
  between operations: 14.1 us -> 0.7 us
  local copies, waits for them, and re-layouts: 1.54 us -> 3.53 us
  other arithmetic: 4.37 us -> 2.45 us
    psum x1 -> x0, waiting for transfers between devices: 70.4 us -> none  [per_device(): owned = lax.psum(owned, 'dp')]
    psum x1 -> x0, blocking collectives: 40.2 us -> none  [per_device(): small = lax.psum(small, ('dp', 'section'))]
    pallas_call x1, Pallas kernels: 30.5 us -> 60.7 us  [all_grads(): pl.pallas_call(functools.partial(kernel, total, dps, secs), out_shape=(ja...]
    all_gather x1 -> x0, blocking collectives: 8.47 us -> none  [per_device(): lax.all_gather(share, 'section', axis=2, tiled=True).reshape(3, 128, 576)]
    unnamed x15, local copies, waits for them, and re-layouts: 1.53 us -> 3.53 us
  transfers between devices with their start and end apart: 2 -> 0, of which waited for: 1 -> 0; matrix products, arithmetic and copies ran while one was open for 1% -> 0% of each run, Pallas kernels for 0% -> 0%
where the time goes in v2:
time: 67.7 us; the launch traced here: 67.4 us
  Pallas kernels  60.7 us (90%)
  local copies, waits for them, and re-layouts  3.53 us (5%)
  other arithmetic  2.45 us (4%)
  between operations  0.7 us (1%)
    pallas_call x1, Pallas kernels, all_grads(): pl.pallas_call(functools.partial(kernel, total, dps, secs), out_shape=(ja...  60.7 us
    unnamed x15, local copies, waits for them, and re-layouts  3.53 us

profile of v2, /device:TPU:0, one launch (start us, length us, event | category | flops | bytes accessed | tf_op | source)
XLA Modules:
  0.0 67.4 jit_solution(3584780991765039924)
XLA Ops:
  0.6 0.0 copy-start.3
  0.6 0.8 %copy.11.hw = f32[64,10]{1,0:T(8,128)S(1)} copy(f32[64,10]{0,1:T(8,128)} %param.12) | data formatting | bytes 5120 | tf_op args[5]
  1.4 0.0 copy-start.2
  1.4 0.0 copy-start.4
  1.4 0.0 copy-start.5
  1.5 0.0 copy-done.3
  1.5 0.7 copy-done.2
  2.1 0.0 copy-done.4
  2.1 0.0 copy-done.5
  2.1 0.0 copy-start
  2.1 0.9 %copy-done = f32[3,2,576,16]{2,3,1,0:T(8,128)S(1)} copy-done((f32[3,2,576,16]{2,3,1,0:T(8,128)S(1)}, f32[3,2,576,16]{2,3,1,0:T(8,128)}, u32[]{:S(2)}) %copy-start) | copy-done | bytes 221208
  3.1 0.0 copy-start.1
  3.1 1.0 %copy-done.1 = bf16[64,4096]{1,0:T(8,128)(2,1)S(1)} copy-done((bf16[64,4096]{1,0:T(8,128)(2,1)S(1)}, bf16[64,4096]{1,0:T(8,128)(2,1)}, u32[]{:S(2)}) %copy-start.1) | copy-done | bytes 524312
  4.1 60.7 %shard_map.102 = (f32[6,16,576]{2,1,0:T(8,128)S(1)}, f32[40,128]{1,0:T(8,128)S(1)}) custom-call(bf16[64,4096]{1,0:T(8,128)(2,1)S(1)} %copy-done.1, s32[1,64]{1,0:T(1,128)S(1)} %bitcast.21, f32[6,16,576]{2,1,0:T(8,128)S(1)} %bitcast.17, f32[3,2,64]{2,1,0:T(2,128)S(1)} %copy-done.2, f32[3,2,64]{2,1,0:T(2,128)S(1)} %copy-done.3, f32[64,10]{1,0:T(8,128)S(1)} %copy.11.hw, ...), custom_call_target="tpu_custom_call" | custom-call | tf_op jit(solution)/shard_map/pallas_call | solution.py:347
  64.9 0.0 copy-start.6
  64.9 0.6 fusion
  65.5 0.1 copy-done.6
  65.6 0.6 bitcast_add_fusion
  66.2 0.5 bitcast_add_fusion.1
  66.7 0.7 %multiply_add_fusion = f32[3,2,576,16]{2,3,1,0:T(8,128)} fusion(f32[3,2,576,16]{2,3,1,0:T(8,128)S(1)} %bitcast.18, f32[3,2,576,16]{2,3,1,0:T(8,128)S(1)} %copy-done), kind=kLoop, calls=%fused_computation | loop fusion | flops 110592 | bytes 663552 | tf_op jit(solution)/shard_map/add | solution.py:393
  (2 shorter events, 0.0 us)
Async XLA Ops:
  0.6 0.8 %copy-start.3 = (f32[3,2,64]{2,1,0:T(2,128)S(1)}, f32[3,2,64]{2,1,0:T(2,128)}, u32[]{:S(2)}) copy-start(f32[3,2,64]{2,1,0:T(2,128)} %bias.1) | copy-start | bytes 4612
  1.4 0.7 %copy-start.2 = (f32[3,2,64]{2,1,0:T(2,128)S(1)}, f32[3,2,64]{2,1,0:T(2,128)}, u32[]{:S(2)}) copy-start(f32[3,2,64]{2,1,0:T(2,128)} %gain.1) | copy-start | bytes 4612
  1.4 0.7 %copy-start.4 = (s32[64]{0:T(128)S(1)}, s32[64]{0:T(128)}, u32[]{:S(2)}) copy-start(s32[64]{0:T(128)} %param.8) | copy-start | bytes 772
  1.4 0.7 %copy-start.5 = (f32[10]{0:T(128)S(1)}, f32[10]{0:T(128)}, u32[]{:S(2)}) copy-start(f32[10]{0:T(128)} %param.13) | copy-start | bytes 124
  2.1 0.9 %copy-start = (f32[3,2,576,16]{2,3,1,0:T(8,128)S(1)}, f32[3,2,576,16]{2,3,1,0:T(8,128)}, u32[]{:S(2)}) copy-start(f32[3,2,576,16]{2,3,1,0:T(8,128)} %param.9) | copy-start | bytes 663556
  3.1 1.0 %copy-start.1 = (bf16[64,4096]{1,0:T(8,128)(2,1)S(1)}, bf16[64,4096]{1,0:T(8,128)(2,1)}, u32[]{:S(2)}) copy-start(bf16[64,4096]{1,0:T(8,128)(2,1)} %img.1) | copy-start | bytes 1572868
  64.9 0.7 %copy-start.6 = (f32[64,10]{0,1:T(8,128)S(1)}, f32[64,10]{0,1:T(8,128)}, u32[]{:S(2)}) copy-start(f32[64,10]{0,1:T(8,128)} %param.12) | copy-start | bytes 7684

commit v3 on v2

--- a/solution.py
+++ b/solution.py
@@ -15,13 +15,23 @@
 OFFSETS = (0, 1, 2, -1)
 
 
-def kernel(total, dps, secs, img, labels, own, gain, bias, hw, hb, conv_out, small,
+CHUNKS = ((5, 4), (3, 2), (1,), (0,))
+
+
+def chunk_tiles(c):
+    return 9 * len(CHUNKS[c]) + (3 if c == 0 else 1)
+
+
+def kernel(total, dps, secs, img_hbm, labels, own_hbm, gain, bias, hw, hb, conv_out, small,
            xs, zs, dsw, rs, wf, wb, qs, qt, du2, du1, hw2, lab, wt, buf, in_a, tot, in_b,
-           fin, w_send, w_recv, a_send, a_recv, b_send, b_recv, c_send, c_recv):
+           fin, img, own, load, w_send, w_recv, a_send, a_recv, b_send, b_recv, c_send, c_recv):
     dp, sec = lax.axis_index("dp"), lax.axis_index("section")
-    tiles = in_a.shape[2]
-    per = in_b.shape[2]
-
+    per = [-(-chunk_tiles(c) // dps) for c in range(len(CHUNKS))]
+
+    load_own = pltpu.make_async_copy(own_hbm, own, load.at[0])
+    load_img = pltpu.make_async_copy(img_hbm, img, load.at[1])
+    load_own.start()
+    load_img.start()
     barrier = pltpu.get_barrier_semaphore()
     for d in range(1, secs):
         pl.semaphore_signal(barrier, inc=1, device_id=(dp, lax.rem(sec + d, secs)),
@@ -33,31 +43,35 @@
         return carry
 
     lax.fori_loop(1, dps, greet, 0)
+    load_own.wait()
     wt[sec] = own[...].astype(BF16)
     pl.semaphore_wait(barrier, secs - 1 + dps - 1)
 
-    def send_w(d):
+    def send_w(b, d):
+        mine = wt.at[sec, pl.ds(2 * b, 2)]
         return pltpu.make_async_remote_copy(
-            src_ref=wt.at[sec], dst_ref=wt.at[sec], send_sem=w_send.at[d - 1],
-            recv_sem=w_recv.at[d - 1], device_id=(dp, lax.rem(sec + d, secs)),
+            src_ref=mine, dst_ref=mine, send_sem=w_send.at[b, d - 1],
+            recv_sem=w_recv.at[b, d - 1], device_id=(dp, lax.rem(sec + d, secs)),
             device_id_type=MESH)
 
     def send_a(b, d):
         to = lax.rem(sec + d, secs)
         return pltpu.make_async_remote_copy(
-            src_ref=buf.at[b, to], dst_ref=in_a.at[b, d - 1], send_sem=a_send.at[b, d - 1],
+            src_ref=buf.at[b, to, pl.ds(0, chunk_tiles(b))],
+            dst_ref=in_a.at[b, d - 1, pl.ds(0, chunk_tiles(b))], send_sem=a_send.at[b, d - 1],
             recv_sem=a_recv.at[b, d - 1], device_id=(dp, to), device_id_type=MESH)
 
     def send_b(b, d):
         to = lax.rem(dp + d, dps)
         return pltpu.make_async_remote_copy(
-            src_ref=tot.at[b, pl.ds(to * per, per)], dst_ref=in_b.at[b, d - 1],
+            src_ref=tot.at[b, pl.ds(to * per[b], per[b])],
+            dst_ref=in_b.at[b, d - 1, pl.ds(0, per[b])],
             send_sem=b_send.at[b, d - 1], recv_sem=b_recv.at[b, d - 1],
             device_id=(to, sec), device_id_type=MESH)
 
     def send_c(b, d):
         to = lax.rem(dp + d, dps)
-        mine = fin.at[b, pl.ds(dp * per, per)]
+        mine = fin.at[b, pl.ds(dp * per[b], per[b])]
         return pltpu.make_async_remote_copy(
             src_ref=mine, dst_ref=mine, send_sem=c_send.at[b, d - 1],
             recv_sem=c_recv.at[b, d - 1], device_id=(to, sec), device_id_type=MESH)
@@ -75,9 +89,10 @@
     def start_b(b):
         for d in range(1, secs):
             send_a(b, d).wait_recv()
-        all_terms = buf[b, sec]
-        for d in range(1, secs):
-            all_terms = all_terms + in_a[b, d - 1]
+        tiles = chunk_tiles(b)
+        all_terms = buf[b, sec, 0:tiles]
+        for d in range(1, secs):
+            all_terms = all_terms + in_a[b, d - 1, 0:tiles]
         tot[b, 0:tiles] = all_terms
         if tot.shape[1] > tiles:
             tot[b, tiles:] = jnp.zeros((tot.shape[1] - tiles, 8, 128), F32)
@@ -85,16 +100,17 @@
 
     def start_c(b):
         each_dp(lambda d: send_b(b, d).wait_recv())
-        sums = lax.fori_loop(1, dps, lambda d, acc: acc + in_b[b, d - 1],
-                             tot[b, pl.ds(dp * per, per)])
-        fin[b, pl.ds(dp * per, per)] = sums
+        sums = lax.fori_loop(1, dps, lambda d, acc: acc + in_b[b, d - 1, 0:per[b]],
+                             tot[b, pl.ds(dp * per[b], per[b])])
+        fin[b, pl.ds(dp * per[b], per[b])] = sums
         each_dp(lambda d: send_c(b, d).start())
 
     def end_c(b):
         each_dp(lambda d: send_c(b, d).wait_recv())
 
-    for d in range(1, secs):
-        send_w(d).start()
+    for b in range(3):
+        for d in range(1, secs):
+            send_w(b, d).start()
     lane = lax.broadcasted_iota(jnp.int32, (1, 128), 1)
     low = lane < 64
 
@@ -133,15 +149,15 @@
     def over_pairs(v):
         return jnp.sum(v.reshape(4, 64, 128), axis=0)
 
+    load_img.wait()
     for y in range(8):
         slab = jnp.stack([img[:, (y * 4 + j) * 128:(y * 4 + j + 1) * 128]
                           for j in range(4)], axis=0).astype(F32)
         put(xs.at[0], y, slab)
 
-    for d in range(1, secs):
-        send_w(d).wait_recv()
-
-    def spread(b, carry):
+    def spread(b):
+        for d in range(1, secs):
+            send_w(b, d).wait_recv()
         flat = jnp.concatenate(
             [wt[q, 2 * b + j] for j in range(2) for q in range(secs)], axis=0).astype(F32)
         zero = jnp.zeros((64, 128), BF16)
@@ -180,13 +196,12 @@
                 for s in range(4):
                     ref[2 * b + j, 768 + s * 64:832 + s * 64, 0:128] = zero
                     ref[2 * b + j, s * 64:s * 64 + 64, 128:256] = zero
-        return carry
-
-    lax.fori_loop(0, 3, spread, 0)
 
     pooled = zero_sum
     for k in range(6):
         b, j = k // 2, k % 2
+        if j == 0:
+            spread(b)
 
         def keep(y, out, energy):
             zs[k, y] = out
@@ -214,14 +229,14 @@
 
     pooled = both(pooled) * (1.0 / 64)
     hw2[...] = jnp.zeros((128, 128), F32)
-    hw2[0:64, 0:hw.shape[1]] = hw[...]
-    hw2[64:128, 0:hw.shape[1]] = hw[...]
+    hw2[0:hw.shape[0], :] = twice(hw[...])
     lab[...] = jnp.zeros((8, 128), jnp.int32)
     lab[0:1, 0:64] = labels[...]
-    classes = hw.shape[1]
+    classes = hw.shape[0]
     hbias = jnp.concatenate([hb[...], jnp.zeros((1, 128 - classes), F32)], axis=1)
-    logits = jnp.dot(jnp.where(low, pooled, 0.0), hw2[...],
-                     precision=lax.Precision.HIGHEST, preferred_element_type=F32) + hbias
+    logits = lax.dot_general(jnp.where(low, pooled, 0.0), hw2[...],
+                             (((1,), (1,)), ((), ())), precision=lax.Precision.HIGHEST,
+                             preferred_element_type=F32) + hbias
     live = lane < classes
     logits = jnp.where(live, logits, -1e30)
     top = jnp.max(logits, axis=1, keepdims=True)
@@ -237,12 +252,10 @@
     row = lax.broadcasted_iota(jnp.int32, (8, 128), 0)
     extra = jnp.where(row == 4, jnp.sum(dl, axis=0, keepdims=True), 0.0)
     for q in range(secs):
-        for b in range(3):
-            buf[b, q, 19] = d_head[0:8] if b == 2 else jnp.zeros((8, 128), F32)
-            buf[b, q, 20] = d_head[8:16] if b == 2 else jnp.zeros((8, 128), F32)
-    spread_g = lax.dot_general(dl, hw2[...], (((1,), (1,)), ((), ())),
-                               precision=lax.Precision.HIGHEST,
-                               preferred_element_type=F32) * (1.0 / 64)
+        buf[0, q, 19] = d_head[0:8]
+        buf[0, q, 20] = d_head[8:16]
+    spread_g = jnp.dot(dl, hw2[...], precision=lax.Precision.HIGHEST,
+                       preferred_element_type=F32) * (1.0 / 64)
     spread_g = spread_g.astype(BF16).astype(F32)
 
     def tally(k, y, d, sums):
@@ -257,14 +270,18 @@
     for k in range(5, -1, -1):
         b, j = k // 2, k % 2
         source = du2 if j == 1 else du1
+        c = [k in ks for ks in CHUNKS].index(True)
+        at_tile = CHUNKS[c].index(k)
+        ends = k == CHUNKS[c][-1]
         r = rs[k]
         dg = both(sums[0]) * r
         db = both(sums[1])
-        extra = jnp.where(row == 2 * j, jnp.sum(dg, axis=0, keepdims=True), extra)
-        extra = jnp.where(row == 2 * j + 1, jnp.sum(db, axis=0, keepdims=True), extra)
-        if j == 0:
+        extra = jnp.where(row == 2 * at_tile, jnp.sum(dg, axis=0, keepdims=True), extra)
+        extra = jnp.where(row == 2 * at_tile + 1, jnp.sum(db, axis=0, keepdims=True), extra)
+        if ends:
             for q in range(secs):
-                buf[b, q, 18] = extra
+                buf[c, q, 9 * len(CHUNKS[c])] = extra
+            extra = jnp.zeros((8, 128), F32)
         c1 = r * twice(gain[b, j:j + 1, :])
         c2 = c1 * dg * r * (1.0 / 64)
 
@@ -292,15 +309,15 @@
                 there = pltpu.roll(here, 64, 1)
                 first, second = (here, there) if e % 2 == 0 else (there, here)
                 for q in range(secs):
-                    buf[b, q, j * 9 + a * 3 + e] = jnp.where(
+                    buf[c, q, at_tile * 9 + a * 3 + e] = jnp.where(
                         low, first[q * 16:q * 16 + 8], second[q * 16 + 8:q * 16 + 16])
 
-        if j == 0:
-            start_a(b)
-        if k <= 3 and j == 1:
-            start_b(b + 1)
-        if k <= 2 and j == 0:
-            start_c(b + 1)
+        if ends:
+            start_a(c)
+        if k == 3:
+            start_b(0)
+        if k == 2:
+            start_c(0)
 
         if j == 1:
             def to_first(y, out, sums):
@@ -309,6 +326,8 @@
                 return tally(k - 1, y, d, sums)
 
             sums = conv(qs, wb.at[k], to_first, (zero_sum, zero_sum))
+            if k == 1:
+                start_b(1)
         elif k > 0:
             def to_second(y, out, sums):
                 g = (du2[y] + out).astype(BF16).astype(F32)
@@ -318,37 +337,44 @@
 
             sums = conv(qs, wb.at[k], to_second, (zero_sum, zero_sum))
 
-    start_b(0)
-    start_c(0)
-    for b in (2, 1, 0):
-        end_c(b)
+    start_c(1)
+    start_b(2)
+    start_b(3)
+    start_c(2)
+    start_c(3)
+    for c, ks in enumerate(CHUNKS):
+        end_c(c)
+        for at_tile, k in enumerate(ks):
+            rows = [fin[c, at_tile * 9 + t] for t in range(9)]
+            conv_out[k, 0:8] = jnp.concatenate([v[:, 0:64] for v in rows], axis=1)
+            conv_out[k, 8:16] = jnp.concatenate([v[:, 64:128] for v in rows], axis=1)
+            small[2 * k:2 * k + 2] = fin[c, 9 * len(ks)][2 * at_tile:2 * at_tile + 2]
+        if c == 0:
+            small[12:13] = fin[c, 18][4:5]
+            small[16:24] = fin[c, 19]
+            small[24:32] = fin[c, 20]
     for b in range(3):
-        for j in range(2):
-            rows = [fin[b, j * 9 + t] for t in range(9)]
-            conv_out[2 * b + j, 0:8] = jnp.concatenate([v[:, 0:64] for v in rows], axis=1)
-            conv_out[2 * b + j, 8:16] = jnp.concatenate([v[:, 64:128] for v in rows], axis=1)
-        small[b * 8:b * 8 + 8] = fin[b, 18]
-    small[24:32] = fin[2, 19]
-    small[32:40] = fin[2, 20]
-    for d in range(1, secs):
-        send_w(d).wait_send()
-    for b in range(3):
-        for d in range(1, secs):
-            send_a(b, d).wait_send()
-        each_dp(lambda d: send_b(b, d).wait_send())
-        each_dp(lambda d: send_c(b, d).wait_send())
+        for d in range(1, secs):
+            send_w(b, d).wait_send()
+    for c in range(len(CHUNKS)):
+        for d in range(1, secs):
+            send_a(c, d).wait_send()
+        each_dp(lambda d: send_b(c, d).wait_send())
+        each_dp(lambda d: send_c(c, d).wait_send())
 
 
 def all_grads(total, dps, secs, images_in, labels, own, gain, bias, hw, hb):
     vmem = pl.BlockSpec(memory_space=pltpu.VMEM)
-    tiles = 21
+    chunks = len(CHUNKS)
+    tiles = max(chunk_tiles(c) for c in range(chunks))
     per = -(-tiles // dps)
+    hbm = pl.BlockSpec(memory_space=pltpu.HBM)
     dma = pltpu.SemaphoreType.DMA
     return pl.pallas_call(
         functools.partial(kernel, total, dps, secs),
         out_shape=(jax.ShapeDtypeStruct(own.shape, F32),
-                   jax.ShapeDtypeStruct((40, 128), F32)),
-        in_specs=[vmem] * 7,
+                   jax.ShapeDtypeStruct((32, 128), F32)),
+        in_specs=[hbm, vmem, hbm, vmem, vmem, vmem, vmem],
         out_specs=(vmem, vmem),
         scratch_shapes=[
             pltpu.VMEM((6, 10, 256, 256), BF16),
@@ -364,15 +390,18 @@
             pltpu.VMEM((128, 128), F32),
             pltpu.VMEM((8, 128), jnp.int32),
             pltpu.VMEM((secs,) + own.shape, BF16),
-            pltpu.VMEM((3, secs, tiles, 8, 128), F32),
-            pltpu.VMEM((3, secs - 1, tiles, 8, 128), F32),
-            pltpu.VMEM((3, per * dps, 8, 128), F32),
-            pltpu.VMEM((3, dps - 1, per, 8, 128), F32),
-            pltpu.VMEM((3, per * dps, 8, 128), F32),
-            dma((secs - 1,)), dma((secs - 1,)),
+            pltpu.VMEM((chunks, secs, tiles, 8, 128), F32),
+            pltpu.VMEM((chunks, secs - 1, tiles, 8, 128), F32),
+            pltpu.VMEM((chunks, per * dps, 8, 128), F32),
+            pltpu.VMEM((chunks, dps - 1, per, 8, 128), F32),
+            pltpu.VMEM((chunks, per * dps, 8, 128), F32),
+            pltpu.VMEM(images_in.shape, BF16),
+            pltpu.VMEM(own.shape, F32),
+            dma((2,)),
             dma((3, secs - 1)), dma((3, secs - 1)),
-            dma((3, dps - 1)), dma((3, dps - 1)),
-            dma((3, dps - 1)), dma((3, dps - 1)),
+            dma((chunks, secs - 1)), dma((chunks, secs - 1)),
+            dma((chunks, dps - 1)), dma((chunks, dps - 1)),
+            dma((chunks, dps - 1)), dma((chunks, dps - 1)),
         ],
         compiler_params=pltpu.CompilerParams(
             vmem_limit_bytes=52 * 1024 * 1024, collective_id=0, has_side_effects=True),
@@ -386,16 +415,16 @@
     own = jnp.swapaxes(conv_weight, 2, 3).reshape(blocks * convs, share, depth)
     owned, small = all_grads(images * dps * secs, dps, secs, images_in,
                              labels.reshape(1, images), own, frn_gain,
-                             frn_bias, head_weight, head_bias.reshape(1, -1))
+                             frn_bias, head_weight.T, head_bias.reshape(1, -1))
     classes = head_bias.shape[0]
     params = jnp.stack([frn_gain, frn_bias], axis=2)
     return (
         jnp.swapaxes(owned.reshape(blocks, convs, share, depth), 2, 3)
         + prior_precision * conv_weight,
-        small[0:24].reshape(3, 8, 128)[:, 0:4, 0:64].reshape(params.shape)
+        small[0:12, 0:64].reshape(params.shape)
         + prior_precision * params,
-        small[24:24 + classes, 0:64].T + prior_precision * head_weight,
-        small[20, 0:classes] + prior_precision * head_bias,
+        small[16:16 + classes, 0:64].T + prior_precision * head_weight,
+        small[12, 0:classes] + prior_precision * head_bias,
     )
 
 

time: 67.7 us -> 66.5 us (0.982)
  Pallas kernels: 60.7 us -> 59.6 us
    pallas_call x1, Pallas kernels: 60.7 us -> 59.6 us  [all_grads(): pl.pallas_call(functools.partial(kernel, total, dps, secs), out_shape=(ja...]
    unnamed x15 -> x18, local copies, waits for them, and re-layouts: 3.53 us -> 3.44 us
where the time goes in v3:
time: 66.5 us; the launch traced here: 66.2 us
  Pallas kernels  59.6 us (90%)
  local copies, waits for them, and re-layouts  3.46 us (5%)
  other arithmetic  2.44 us (4%)
  between operations  0.7 us (1%)
    pallas_call x1, Pallas kernels, all_grads(): pl.pallas_call(functools.partial(kernel, total, dps, secs), out_shape=(ja...  59.6 us
    unnamed x18, local copies, waits for them, and re-layouts  3.44 us

profile of v3, /device:TPU:0, one launch (start us, length us, event | category | flops | bytes accessed | tf_op | source)
XLA Modules:
  0.0 66.2 jit_solution(17903939653564551990)
XLA Ops:
  0.6 0.0 copy-start.6
  0.6 0.0 copy-start.5
  0.7 0.0 copy-start.7
  0.7 0.0 copy-start.8
  0.7 0.6 copy-done.6
  1.3 0.0 copy-done.5
  1.3 0.0 copy-done.7
  1.3 0.0 copy-done.8
  1.3 0.0 copy-start
  1.3 0.9 %copy-done = f32[3,2,576,16]{2,3,1,0:T(8,128)S(1)} copy-done((f32[3,2,576,16]{2,3,1,0:T(8,128)S(1)}, f32[3,2,576,16]{2,3,1,0:T(8,128)}, u32[]{:S(2)}) %copy-start) | copy-done | bytes 221208
  2.3 0.0 copy-start.2
  2.3 1.0 %copy-done.2 = bf16[64,4096]{1,0:T(8,128)(2,1)S(1)} copy-done((bf16[64,4096]{1,0:T(8,128)(2,1)S(1)}, bf16[64,4096]{1,0:T(8,128)(2,1)}, u32[]{:S(2)}) %copy-start.2) | copy-done | bytes 524312
  3.3 0.0 copy-start.3
  3.3 0.7 %copy-done.3 = f32[64,10]{0,1:T(8,128)S(1)} copy-done((f32[64,10]{0,1:T(8,128)S(1)}, f32[64,10]{0,1:T(8,128)}, u32[]{:S(2)}) %copy-start.3) | copy-done | bytes 2584
  4.0 0.0 copy-start.1
  4.0 59.6 %shard_map.102 = (f32[6,16,576]{2,1,0:T(8,128)S(1)}, f32[32,128]{1,0:T(8,128)S(1)}) custom-call(bf16[64,4096]{1,0:T(8,128)(2,1)S(1)} %copy-done.2, s32[1,64]{1,0:T(1,128)S(1)} %bitcast.20, f32[6,16,576]{2,1,0:T(8,128)S(1)} %bitcast.15, f32[3,2,64]{2,1,0:T(2,128)S(1)} %copy-done.5, f32[3,2,64]{2,1,0:T(2,128)S(1)} %copy-done.6, f32[10,64]{1,0:T(8,128)S(1)} %bitcast.17, ...), custom_call_target="tpu_custom_call" | custom-call | tf_op jit(solution)/shard_map/pallas_call | solution.py:373
  63.7 0.0 copy-start.4
  63.7 0.6 fusion
  64.3 0.1 copy-done.4
  64.4 0.6 bitcast_add_fusion
  65.0 0.5 bitcast_add_fusion.1
  65.5 0.0 copy-done.1
  65.5 0.7 %multiply_add_fusion = f32[3,2,576,16]{2,3,1,0:T(8,128)} fusion(f32[3,2,576,16]{2,3,1,0:T(8,128)S(1)} %bitcast.16, f32[3,2,576,16]{2,3,1,0:T(8,128)S(1)} %copy-done.1), kind=kLoop, calls=%fused_computation | loop fusion | flops 110592 | bytes 663552 | tf_op jit(solution)/shard_map/add | solution.py:422
  (2 shorter events, 0.0 us)
Async XLA Ops:
  0.6 0.7 %copy-start.6 = (f32[3,2,64]{2,1,0:T(2,128)S(1)}, f32[3,2,64]{2,1,0:T(2,128)}, u32[]{:S(2)}) copy-start(f32[3,2,64]{2,1,0:T(2,128)} %bias.1) | copy-start | bytes 4612
  0.6 0.7 %copy-start.5 = (f32[3,2,64]{2,1,0:T(2,128)S(1)}, f32[3,2,64]{2,1,0:T(2,128)}, u32[]{:S(2)}) copy-start(f32[3,2,64]{2,1,0:T(2,128)} %gain.1) | copy-start | bytes 4612
  0.7 0.7 %copy-start.7 = (s32[64]{0:T(128)S(1)}, s32[64]{0:T(128)}, u32[]{:S(2)}) copy-start(s32[64]{0:T(128)} %param.8) | copy-start | bytes 772
  0.7 0.7 %copy-start.8 = (f32[10]{0:T(128)S(1)}, f32[10]{0:T(128)}, u32[]{:S(2)}) copy-start(f32[10]{0:T(128)} %param.13) | copy-start | bytes 124
  1.3 0.9 %copy-start = (f32[3,2,576,16]{2,3,1,0:T(8,128)S(1)}, f32[3,2,576,16]{2,3,1,0:T(8,128)}, u32[]{:S(2)}) copy-start(f32[3,2,576,16]{2,3,1,0:T(8,128)} %param.9) | copy-start | bytes 663556
  2.3 1.0 %copy-start.2 = (bf16[64,4096]{1,0:T(8,128)(2,1)S(1)}, bf16[64,4096]{1,0:T(8,128)(2,1)}, u32[]{:S(2)}) copy-start(bf16[64,4096]{1,0:T(8,128)(2,1)} %img_hbm.1) | copy-start | bytes 1572868
  3.3 0.7 %copy-start.3 = (f32[64,10]{0,1:T(8,128)S(1)}, f32[64,10]{0,1:T(8,128)}, u32[]{:S(2)}) copy-start(f32[64,10]{0,1:T(8,128)} %param.12) | copy-start | bytes 7684
  4.0 61.5 %copy-start.1 = (f32[3,2,576,16]{2,3,1,0:T(8,128)S(1)}, f32[3,2,576,16]{2,3,1,0:T(8,128)}, u32[]{:S(2)}) copy-start(f32[3,2,576,16]{2,3,1,0:T(8,128)} %param.9) | copy-start | bytes 663556
  63.7 0.7 %copy-start.4 = (f32[64,10]{0,1:T(8,128)S(1)}, f32[64,10]{0,1:T(8,128)}, u32[]{:S(2)}) copy-start(f32[64,10]{0,1:T(8,128)} %param.12) | copy-start | bytes 7684

commit v4 on v3

--- a/solution.py
+++ b/solution.py
@@ -404,7 +404,7 @@
             dma((chunks, dps - 1)), dma((chunks, dps - 1)),
         ],
         compiler_params=pltpu.CompilerParams(
-            vmem_limit_bytes=52 * 1024 * 1024, collective_id=0, has_side_effects=True),
+            vmem_limit_bytes=63 * 1024 * 1024 + 768 * 1024, collective_id=0, has_side_effects=True),
     )(images_in, labels, own, gain, bias, hw, hb)
 
 

time: 66.5 us -> 66 us (level)
  local copies, waits for them, and re-layouts: 3.46 us -> 0.87 us
  other arithmetic: 2.44 us -> 3.5 us
  Pallas kernels: 59.6 us -> 60.6 us
    unnamed x18 -> x10, local copies, waits for them, and re-layouts: 3.44 us -> 0.16 us
    add x1, other arithmetic: 0.72 us -> 1.78 us  [per_device(): jnp.swapaxes(owned.reshape(blocks, convs, share, depth), 2, 3)]
    pallas_call x1, Pallas kernels: 59.6 us -> 60.6 us  [all_grads(): pl.pallas_call(functools.partial(kernel, total, dps, secs), out_shape=(ja...]
    slice x1, local copies, waits for them, and re-layouts: 0.01 us -> 0.71 us  [per_device(): small[0:12, 0:64].reshape(params.shape) + prior_precision * params]
where the time goes in v4:
time: 66 us; the launch traced here: 65.7 us
  Pallas kernels  60.6 us (92%)
  other arithmetic  3.5 us (5%)
  local copies, waits for them, and re-layouts  0.87 us (1%)
  between operations  0.68 us (1%)
    pallas_call x1, Pallas kernels, all_grads(): pl.pallas_call(functools.partial(kernel, total, dps, secs), out_shape=(ja...  60.6 us
    add x1, other arithmetic, per_device(): jnp.swapaxes(owned.reshape(blocks, convs, share, depth), 2, 3)  1.78 us

profile of v4, /device:TPU:0, one launch (start us, length us, event | category | flops | bytes accessed | tf_op | source)
XLA Modules:
  0.0 65.7 jit_solution(4855034968180427687)
XLA Ops:
  0.6 60.6 %shard_map.102 = (f32[6,16,576]{2,1,0:T(8,128)}, f32[32,128]{1,0:T(8,128)}) custom-call(bf16[64,4096]{1,0:T(8,128)(2,1)} %img_hbm.1, s32[1,64]{1,0:T(1,128)} %bitcast.20, f32[6,16,576]{2,1,0:T(8,128)} %bitcast.15, f32[3,2,64]{2,1,0:T(2,128)} %gain.1, f32[3,2,64]{2,1,0:T(2,128)} %bias.1, f32[10,64]{1,0:T(8,128)} %bitcast.17, f32[1,10]{1,0:T(1,128)} %bitcast.21), custom_call_target="tpu_custom_call" | custom-call | tf_op jit(solution)/shard_map/pallas_call | solution.py:373
  61.2 0.0 copy-start.2
  61.2 0.0 copy-start.3
  61.3 0.7 %slice.9 = f32[12,64]{1,0:T(8,128)S(1)} slice(f32[32,128]{1,0:T(8,128)} %get-tuple-element.7), slice={[0:12], [0:64]} | slice | bytes 6144 | tf_op jit(solution)/shard_map/slice | solution.py:424
  62.0 0.0 copy-start.1
  62.0 0.0 copy-done.2
  62.0 0.0 copy-done.3
  62.0 0.0 copy-start
  62.0 0.6 fusion
  62.6 0.1 copy-done.1
  62.7 0.0 copy-done
  62.7 0.0 copy-start.4
  62.7 0.6 bitcast_add_fusion
  63.3 0.1 copy-done.4
  63.4 0.5 bitcast_add_fusion.1
  63.9 1.8 %multiply_add_fusion = f32[3,2,576,16]{2,3,1,0:T(8,128)} fusion(f32[3,2,576,16]{2,3,1,0:T(8,128)} %bitcast.16, f32[3,2,576,16]{2,3,1,0:T(8,128)} %param.9), kind=kLoop, calls=%fused_computation | loop fusion | flops 110592 | bytes 663552 | tf_op jit(solution)/shard_map/add | solution.py:422
  (1 shorter events, 0.0 us)
Async XLA Ops:
  61.2 0.7 %copy-start.2 = (f32[3,2,64]{2,1,0:T(2,128)S(1)}, f32[3,2,64]{2,1,0:T(2,128)}, u32[]{:S(2)}) copy-start(f32[3,2,64]{2,1,0:T(2,128)} %gain.1) | copy-start | bytes 4612
  61.2 0.7 %copy-start.3 = (f32[3,2,64]{2,1,0:T(2,128)S(1)}, f32[3,2,64]{2,1,0:T(2,128)}, u32[]{:S(2)}) copy-start(f32[3,2,64]{2,1,0:T(2,128)} %bias.1) | copy-start | bytes 4612
  62.0 0.7 %copy-start.1 = (f32[32,128]{1,0:T(8,128)S(1)}, f32[32,128]{1,0:T(8,128)}, u32[]{:S(2)}) copy-start(f32[32,128]{1,0:T(8,128)} %get-tuple-element.7) | copy-start | bytes 49156
  62.0 0.7 %copy-start = (f32[64,10]{0,1:T(8,128)S(1)}, f32[64,10]{0,1:T(8,128)}, u32[]{:S(2)}) copy-start(f32[64,10]{0,1:T(8,128)} %param.12) | copy-start | bytes 7684
  62.7 0.7 %copy-start.4 = (f32[10]{0:T(128)S(1)}, f32[10]{0:T(128)}, u32[]{:S(2)}) copy-start(f32[10]{0:T(128)} %param.13) | copy-start | bytes 124
